TPU v7x, 32 devices: a whole 2x2x4 slice. The times are simulated.
32 devices in a mesh: groups: 2 (over x), dp: 16 (over z, y, core).
Axes of the slice: x: 2, y: 2, z: 4, core: 2. Of those that a mesh axis runs over, the one named last changes fastest.
Arguments:
- queries: bfloat16 [4096, 2048], P(('groups', 'dp')), parts along dimension 0, may hold values from -6 to 6
- key_vectors: bfloat16 [4096, 512], P(('groups', 'dp')), parts along dimension 0, may hold values from -6 to 6
- value_vectors: bfloat16 [4096, 512], P(('groups', 'dp')), parts along dimension 0, may hold values from -6 to 6
- output_gradient: bfloat16 [4096, 2048], P(('groups', 'dp')), parts along dimension 0, may hold values from -6 to 6
- doc_lengths: int32 [16], P('groups'), parts along dimension 0, may hold values from 1 to 512, 2048 in all
Outputs:
- attention_result: bfloat16 [4096, 2048], P(('groups', 'dp')), parts along dimension 0
- query_gradient: bfloat16 [4096, 2048], P(('groups', 'dp')), parts along dimension 0
- grad_k: bfloat16 [4096, 512], P(('groups', 'dp')), parts along dimension 0
- grad_v: bfloat16 [4096, 512], P(('groups', 'dp')), parts along dimension 0
There are 2 independent parts, one for each index of `groups`. A program takes and returns all parts, laid end to end along the dimension named above; each array names one. Nothing has to cross between parts.
Inputs may be any that keep to these rules, and one draw needn't show every extreme that they name: `doc_lengths`: the lengths sum to 2048; the longest document has exactly 512 tokens.
All inputs are finite; a program needn't handle non-finite values.
Results may differ from a plain program's by a relative error of at most 0.012.
Values may be sent and summed in bfloat16 or wider, within the bound.
A program may use at most 64 MiB of HBM per device.

v0:
```python
import math

import jax
import jax.numpy as jnp
from jax import lax
from jax.sharding import PartitionSpec as P

HEAD_WIDTH = 128
QUERY_HEADS = 16
KEY_VALUE_HEADS = 4
SPAN = 4


masked_score = -1e30


def passed_along(value, axis, steps):
    count = lax.axis_size(axis)
    first, last = (max(0, -steps), min(count, count - steps))
    return lax.ppermute(value, axis, [(source, source + steps) for source in range(first, last)])


def segment_ids(doc_ends, positions):
    return jnp.sum((doc_ends[None, :] <= positions[:, None]).astype(jnp.int32), axis=1)


def head_slice(matrix, head_cluster, size):
    return matrix[:, head_cluster * size : (head_cluster + 1) * size]


def score_grads(
    query_part, grad_part, log_sums, delta_rows, key_part, value_part, allowed, score_scale
):
    scores = (
        jnp.einsum("qjd,kd->jqk", query_part, key_part, preferred_element_type=jnp.float32)
        * score_scale
    )
    probs = jnp.where(allowed[None], jnp.exp(scores - log_sums.T[:, :, None]), 0.0)
    prob_grads = jnp.einsum(
        "qjd,kd->jqk", grad_part, value_part, preferred_element_type=jnp.float32
    )
    score_grad = (probs * (prob_grads - delta_rows.T[:, :, None])).astype(jnp.bfloat16)
    return (score_grad, probs.astype(jnp.bfloat16))


def body(queries, key_vectors, value_vectors, output_gradient, doc_lengths):
    row_count = queries.shape[0]
    group_width = QUERY_HEADS // KEY_VALUE_HEADS
    group_cols = group_width * HEAD_WIDTH
    score_scale = 1.0 / math.sqrt(HEAD_WIDTH)
    device_index = lax.axis_index("dp")
    doc_ends = jnp.cumsum(doc_lengths)
    stream_end = doc_ends[-1]
    local_pos = device_index * row_count + jnp.arange(row_count)
    local_seg = segment_ids(doc_ends, local_pos)
    reach = SPAN * row_count
    window = reach + row_count
    before_pos = local_pos[0] - reach + jnp.arange(window)
    before_seg = segment_ids(doc_ends, before_pos)
    allowed = (
        (before_pos[None, :] <= local_pos[:, None])
        & (before_seg[None, :] == local_seg[:, None])
        & (before_pos[None, :] >= 0)
    )
    fetched = [
        passed_along((key_vectors, value_vectors), "dp", offset) for offset in range(SPAN, 0, -1)
    ]
    key_window = jnp.concatenate([piece[0] for piece in fetched] + [key_vectors], axis=0)
    value_window = jnp.concatenate([piece[1] for piece in fetched] + [value_vectors], axis=0)
    mixed_parts = []
    log_parts = []
    for head_cluster in range(KEY_VALUE_HEADS):
        query_part = head_slice(queries, head_cluster, group_cols).reshape(
            row_count, group_width, HEAD_WIDTH
        )
        scores = (
            jnp.einsum(
                "qjd,kd->jqk",
                query_part,
                head_slice(key_window, head_cluster, HEAD_WIDTH),
                preferred_element_type=jnp.float32,
            )
            * score_scale
        )
        scores = jnp.where(allowed[None], scores, masked_score)
        row_max = jnp.max(scores, axis=-1, keepdims=True)
        weights = jnp.where(allowed[None], jnp.exp(scores - row_max), 0.0)
        weight_sum = jnp.sum(weights, axis=-1, keepdims=True)
        mixed_rows = jnp.einsum(
            "jqk,kd->qjd",
            weights.astype(jnp.bfloat16),
            head_slice(value_window, head_cluster, HEAD_WIDTH),
            preferred_element_type=jnp.float32,
        )
        mixed_rows = mixed_rows / jnp.transpose(weight_sum, (1, 0, 2))
        mixed_parts.append(mixed_rows.astype(jnp.bfloat16).reshape(row_count, group_cols))
        log_parts.append((row_max + jnp.log(weight_sum))[..., 0].T)
    attention_result = jnp.concatenate(mixed_parts, axis=1)
    logsum_total = jnp.concatenate(log_parts, axis=1)
    delta_all = jnp.sum(
        (output_gradient.astype(jnp.float32) * attention_result.astype(jnp.float32)).reshape(
            row_count, QUERY_HEADS, HEAD_WIDTH
        ),
        axis=-1,
    )
    query_grads = []
    key_gradients = []
    value_gradients = []
    again = [
        passed_along((key_vectors, value_vectors), "dp", offset) for offset in range(SPAN, 0, -1)
    ]
    key_again = jnp.concatenate([piece[0] for piece in again] + [key_vectors], axis=0)
    value_again = jnp.concatenate([piece[1] for piece in again] + [value_vectors], axis=0)
    for head_cluster in range(KEY_VALUE_HEADS):
        query_part = head_slice(queries, head_cluster, group_cols).reshape(
            row_count, group_width, HEAD_WIDTH
        )
        grad_part = head_slice(output_gradient, head_cluster, group_cols).reshape(
            row_count, group_width, HEAD_WIDTH
        )
        key_part = head_slice(key_again, head_cluster, HEAD_WIDTH)
        score_grad, probs16 = score_grads(
            query_part,
            grad_part,
            head_slice(logsum_total, head_cluster, group_width),
            head_slice(delta_all, head_cluster, group_width),
            key_part,
            head_slice(value_again, head_cluster, HEAD_WIDTH),
            allowed,
            score_scale,
        )
        query_grad = (
            jnp.einsum("jqk,kd->qjd", score_grad, key_part, preferred_element_type=jnp.float32)
            * score_scale
        )
        query_grads.append(query_grad.astype(jnp.bfloat16).reshape(row_count, group_cols))
    later = [
        passed_along((queries, output_gradient), "dp", -offset) for offset in range(1, SPAN + 1)
    ]
    later_stats = [
        passed_along((logsum_total, delta_all), "dp", -offset) for offset in range(1, SPAN + 1)
    ]
    query_window = jnp.concatenate([queries] + [piece[0] for piece in later], axis=0)
    grad_window = jnp.concatenate([output_gradient] + [piece[1] for piece in later], axis=0)
    log_window = jnp.concatenate([logsum_total] + [piece[0] for piece in later_stats], axis=0)
    delta_window = jnp.concatenate([delta_all] + [piece[1] for piece in later_stats], axis=0)
    after_pos = local_pos[0] + jnp.arange(window)
    after_seg = segment_ids(doc_ends, after_pos)
    allowed_after = (
        (after_pos[:, None] >= local_pos[None, :])
        & (after_seg[:, None] == local_seg[None, :])
        & (after_pos[:, None] < stream_end)
    )
    for head_cluster in range(KEY_VALUE_HEADS):
        query_part = head_slice(query_window, head_cluster, group_cols).reshape(
            window, group_width, HEAD_WIDTH
        )
        grad_part = head_slice(grad_window, head_cluster, group_cols).reshape(
            window, group_width, HEAD_WIDTH
        )
        score_grad, probs16 = score_grads(
            query_part,
            grad_part,
            head_slice(log_window, head_cluster, group_width),
            head_slice(delta_window, head_cluster, group_width),
            head_slice(key_vectors, head_cluster, HEAD_WIDTH),
            head_slice(value_vectors, head_cluster, HEAD_WIDTH),
            allowed_after,
            score_scale,
        )
        key_gradients.append(
            jnp.einsum("jqk,qjd->kd", score_grad, query_part, preferred_element_type=jnp.float32)
            * score_scale
        )
        value_gradients.append(
            jnp.einsum("jqk,qjd->kd", probs16, grad_part, preferred_element_type=jnp.float32)
        )
    grad_k = jnp.concatenate(key_gradients, axis=1).astype(jnp.bfloat16)
    grad_v = jnp.concatenate(value_gradients, axis=1).astype(jnp.bfloat16)
    query_gradient = jnp.concatenate(query_grads, axis=1)
    return (attention_result, query_gradient, grad_k, grad_v)


def solution(mesh):
    return jax.shard_map(
        body,
        mesh=mesh,
        in_specs=(
            P(("groups", "dp"), None),
            P(("groups", "dp"), None),
            P(("groups", "dp"), None),
            P(("groups", "dp"), None),
            P("groups"),
        ),
        out_specs=(
            P(("groups", "dp"), None),
            P(("groups", "dp"), None),
            P(("groups", "dp"), None),
            P(("groups", "dp"), None),
        ),
        check_vma=False,
    )
```

profile of v0, /device:TPU:0, one launch (start us, length us, event | category | flops | bytes accessed | tf_op | source)
XLA Modules:
  0.0 187.4 jit_solution(10270440208657907224)
XLA Ops:
  0.6 4.9 %collective-permute-start.4 = (bf16[128,512]{1,0:T(8,128)(2,1)}, bf16[128,512]{1,0:T(8,128)(2,1)S(1)}, u32[]{:S(2)}, u32[]{:S(2)}) collective-permute-start(bf16[128,512]{1,0:T(8,128)(2,1)} %param.6), channel_id=1, source_target_pairs={{0,4},{1,5},{2,6},{3,7},{4,8},{5,9},{6,10},{7,11},{8,12},{9,13},{1... | collective-permute-start | bytes 393224 | tf_op jit(solution)/shard_map/ppermute | solution.py:20
  5.6 2.6 %collective-permute-start.5 = (bf16[128,512]{1,0:T(8,128)(2,1)}, bf16[128,512]{1,0:T(8,128)(2,1)S(1)}, u32[]{:S(2)}, u32[]{:S(2)}) collective-permute-start(bf16[128,512]{1,0:T(8,128)(2,1)} %param.6), channel_id=1, source_target_pairs={{0,3},{1,4},{2,5},{3,6},{4,7},{5,8},{6,9},{7,10},{8,11},{9,12},{10... | collective-permute-start | bytes 393224 | tf_op jit(solution)/shard_map/ppermute | solution.py:20
  8.2 3.4 %collective-permute-start.6 = (bf16[128,512]{1,0:T(8,128)(2,1)}, bf16[128,512]{1,0:T(8,128)(2,1)S(1)}, u32[]{:S(2)}, u32[]{:S(2)}) collective-permute-start(bf16[128,512]{1,0:T(8,128)(2,1)} %param.6), channel_id=1, source_target_pairs={{0,2},{1,3},{2,4},{3,5},{4,6},{5,7},{6,8},{7,9},{8,10},{9,11},{10,... | collective-permute-start | bytes 393224 | tf_op jit(solution)/shard_map/ppermute | solution.py:20
  11.6 2.6 %collective-permute-start.7 = (bf16[128,512]{1,0:T(8,128)(2,1)}, bf16[128,512]{1,0:T(8,128)(2,1)S(1)}, u32[]{:S(2)}, u32[]{:S(2)}) collective-permute-start(bf16[128,512]{1,0:T(8,128)(2,1)} %param.6), channel_id=1, source_target_pairs={{0,1},{1,2},{2,3},{3,4},{4,5},{5,6},{6,7},{7,8},{8,9},{9,10},{10,1... | collective-permute-start | bytes 393224 | tf_op jit(solution)/shard_map/ppermute | solution.py:20
  15.3 4.1 %collective-permute-start = (bf16[128,512]{0,1:T(8,128)(2,1)S(1)}, bf16[128,512]{0,1:T(8,128)(2,1)}, u32[]{:S(2)}, u32[]{:S(2)}) collective-permute-start(bf16[128,512]{0,1:T(8,128)(2,1)S(1)} %copy.299), channel_id=1, source_target_pairs={{0,4},{1,5},{2,6},{3,7},{4,8},{5,9},{6,10},{7,11},{8,12},{9,13},{1... | collective-permute-start | bytes 393224 | tf_op jit(solution)/shard_map/ppermute | solution.py:20
  19.6 2.1 %copy.304 = bf16[128,2048]{0,1:T(8,128)(2,1)} copy(bf16[128,2048]{1,0:T(8,128)(2,1)} %param.5) | data formatting | bytes 1048576 | tf_op args[0]
  30.3 3.0 %collective-permute-start.1 = (bf16[128,512]{0,1:T(8,128)(2,1)S(1)}, bf16[128,512]{0,1:T(8,128)(2,1)S(1)}, u32[]{:S(2)}, u32[]{:S(2)}) collective-permute-start(bf16[128,512]{0,1:T(8,128)(2,1)S(1)} %copy.299), channel_id=1, source_target_pairs={{0,3},{1,4},{2,5},{3,6},{4,7},{5,8},{6,9},{7,10},{8,11},{9,12},{10... | collective-permute-start | bytes 393224 | tf_op jit(solution)/shard_map/ppermute | solution.py:20
  33.3 2.3 %collective-permute-start.2 = (bf16[128,512]{0,1:T(8,128)(2,1)S(1)}, bf16[128,512]{0,1:T(8,128)(2,1)S(1)}, u32[]{:S(2)}, u32[]{:S(2)}) collective-permute-start(bf16[128,512]{0,1:T(8,128)(2,1)S(1)} %copy.299), channel_id=1, source_target_pairs={{0,2},{1,3},{2,4},{3,5},{4,6},{5,7},{6,8},{7,9},{8,10},{9,11},{10,... | collective-permute-start | bytes 393224 | tf_op jit(solution)/shard_map/ppermute | solution.py:20
  50.0 2.5 %fusion.61 = bf16[128,4,128]{0,2,1:T(8,128)(2,1)} fusion(f32[4,128,640]{1,2,0:T(8,128)} %copy-done.7, f32[4,128]{1,0:T(4,128)S(1)} %get-tuple-element.29, pred[128,640]{0,1:T(8,128)(4,1)S(1)} %and_and_fusion.1, f32[128,4]{0,1:T(4,128)S(1)} %bitcast.448, bf16[640,512]{0,1:T(8,128)(2,1)} %copy-done.20), kind=kOutput, calls=%fused_computation.89 | convolution fusion | flops 85327872 | bytes 1691648 | tf_op jit(solution)/shard_map/jqk,kd->qjd/dot_general | solution.py:89
  54.7 2.5 %fusion.60 = bf16[128,4,128]{0,2,1:T(8,128)(2,1)} fusion(f32[4,128,640]{1,2,0:T(8,128)} %copy-done.9, f32[4,128]{1,0:T(4,128)S(1)} %get-tuple-element.69, pred[128,640]{0,1:T(8,128)(4,1)S(1)} %and_and_fusion.1, f32[128,4]{0,1:T(4,128)S(1)} %bitcast.455, bf16[640,512]{0,1:T(8,128)(2,1)} %copy-done.20), kind=kOutput, calls=%fused_computation.88 | convolution fusion | flops 85327872 | bytes 1691648 | tf_op jit(solution)/shard_map/jqk,kd->qjd/dot_general | solution.py:89
  58.9 2.0 %multiply_bitcast_fusion = (f32[16,8,16,128]{3,1,2,0:T(8,128)S(1)}, bf16[128,2048]{1,0:T(8,128)(2,1)}) fusion(bf16[128,2048]{1,0:T(8,128)(2,1)} %param.8, bf16[128,512]{1,0:T(8,128)(2,1)S(1)} %copy.319, bf16[128,512]{1,0:T(8,128)(2,1)S(1)} %copy.318, bf16[128,512]{1,0:T(8,128)(2,1)} %copy.317, bf16[128,512]{1,0:T(8,128)(2,1)} %copy.316), kind=kLoop, calls=%fused_computation.116 | loop fusion | flops 2883584 | bytes 2621440
  67.8 2.4 %fusion.64 = bf16[128,4,128]{2,0,1:T(8,128)(2,1)} fusion(bf16[128,4,128]{0,2,1:T(8,128)(2,1)} %bitcast.443, f32[4,128,640]{1,2,0:T(8,128)S(1)} %fusion.4, f32[4,128]{1,0:T(4,128)S(1)} %copy.341, f32[4,128]{1,0:T(4,128)S(1)} %copy-done.22, pred[128,640]{0,1:T(8,128)(4,1)S(1)} %and_and_fusion.1, bf16[640,512]{0,1:T(8,128)(2,1)} %copy-done.20, ...), kind=kOutput, calls=%fused_computation.92 | convolution fusion | flops 169541632 | bytes 1986560 | tf_op jit(solution)/shard_map/jqk,kd->qjd/dot_general | solution.py:133
  71.2 2.5 %fusion.65 = bf16[128,4,128]{2,0,1:T(8,128)(2,1)} fusion(bf16[128,4,128]{0,2,1:T(8,128)(2,1)} %bitcast.442, f32[4,128,640]{1,2,0:T(8,128)S(1)} %fusion.5, f32[4,128]{1,0:T(4,128)S(1)} %copy.335, f32[4,128]{1,0:T(4,128)S(1)} %copy-done.24, pred[128,640]{0,1:T(8,128)(4,1)S(1)} %and_and_fusion.1, bf16[640,512]{0,1:T(8,128)(2,1)} %copy-done.20, ...), kind=kOutput, calls=%fused_computation.93 | convolution fusion | flops 169541632 | bytes 1986560 | tf_op jit(solution)/shard_map/jqk,kd->qjd/dot_general | solution.py:133
  78.8 2.9 %fusion.67 = bf16[128,4,128]{2,0,1:T(8,128)(2,1)} fusion(bf16[128,4,128]{0,2,1:T(8,128)(2,1)} %bitcast.440, f32[4,128,640]{1,2,0:T(8,128)} %copy-done.9, f32[4,128]{1,0:T(4,128)} %copy.323, f32[4,128]{1,0:T(4,128)} %get-tuple-element.75, pred[128,640]{0,1:T(8,128)(4,1)S(1)} %and_and_fusion.1, bf16[640,512]{0,1:T(8,128)(2,1)} %copy-done.20, ...), kind=kOutput, calls=%fused_computation.95 | convolution fusion | flops 169541632 | bytes 1986560 | tf_op jit(solution)/shard_map/jqk,kd->qjd/dot_general | solution.py:133
  89.7 5.0 %collective-permute-done.22 = f32[128,16]{1,0:T(8,128)S(1)} collective-permute-done((f32[128,16]{1,0:T(8,128)S(1)}, f32[128,16]{1,0:T(8,128)S(1)}, u32[]{:S(2)}, u32[]{:S(2)}) %collective-permute-start.22) | collective-permute-done | bytes 8224 | tf_op jit(solution)/shard_map/ppermute | solution.py:20
  97.4 4.7 %collective-permute-done.13 = f32[128,16]{0,1:T(8,128)S(1)} collective-permute-done((f32[128,16]{0,1:T(8,128)S(1)}, f32[128,16]{0,1:T(8,128)S(1)}, u32[]{:S(2)}, u32[]{:S(2)}) %collective-permute-start.13) | collective-permute-done | bytes 8224 | tf_op jit(solution)/shard_map/ppermute | solution.py:20
  105.0 6.3 %collective-permute-done.23 = f32[128,16]{1,0:T(8,128)S(1)} collective-permute-done((f32[128,16]{1,0:T(8,128)S(1)}, f32[128,16]{1,0:T(8,128)S(1)}, u32[]{:S(2)}, u32[]{:S(2)}) %collective-permute-start.23) | collective-permute-done | bytes 8224 | tf_op jit(solution)/shard_map/ppermute | solution.py:20
  122.9 6.3 %collective-permute-done.11 = bf16[128,2048]{0,1:T(8,128)(2,1)} collective-permute-done((bf16[128,2048]{0,1:T(8,128)(2,1)}, bf16[128,2048]{0,1:T(8,128)(2,1)}, u32[]{:S(2)}, u32[]{:S(2)}) %collective-permute-start.11) | collective-permute-done | bytes 524320 | tf_op jit(solution)/shard_map/ppermute | solution.py:20
  130.6 7.7 %collective-permute-done.17 = bf16[128,2048]{0,1:T(8,128)(2,1)S(1)} collective-permute-done((bf16[128,2048]{0,1:T(8,128)(2,1)S(1)}, bf16[128,2048]{0,1:T(8,128)(2,1)S(1)}, u32[]{:S(2)}, u32[]{:S(2)}) %collective-permute-start.17) | collective-permute-done | bytes 524320 | tf_op jit(solution)/shard_map/ppermute | solution.py:20
  138.4 2.9 %collective-permute-done.18 = bf16[128,2048]{0,1:T(8,128)(2,1)S(1)} collective-permute-done((bf16[128,2048]{0,1:T(8,128)(2,1)S(1)}, bf16[128,2048]{0,1:T(8,128)(2,1)S(1)}, u32[]{:S(2)}, u32[]{:S(2)}) %collective-permute-start.18) | collective-permute-done | bytes 524320 | tf_op jit(solution)/shard_map/ppermute | solution.py:20
  142.8 25.3 %collective-permute-done.19 = bf16[128,2048]{0,1:T(8,128)(2,1)S(1)} collective-permute-done((bf16[128,2048]{0,1:T(8,128)(2,1)S(1)}, bf16[128,2048]{0,1:T(8,128)(2,1)S(1)}, u32[]{:S(2)}, u32[]{:S(2)}) %collective-permute-start.19) | collective-permute-done | bytes 524320 | tf_op jit(solution)/shard_map/ppermute | solution.py:20
  172.1 2.1 %fusion.79 = bf16[128,128]{0,1:T(8,128)(2,1)S(1)} fusion(bf16[640,4,128]{0,2,1:T(8,128)(2,1)S(1)} %bitcast.428, f32[4,640,128]{2,1,0:T(8,128)} %copy-done, bf16[640,4,128]{0,2,1:T(8,128)(2,1)S(1)} %bitcast.419, f32[4,640]{1,0:T(4,128)S(1)} %get-tuple-element.60, bf16[128,512]{1,0:T(8,128)(2,1)S(1)} %copy-done.11), kind=kOutput, calls=%fused_computation.111 | convolution fusion | flops 168787968 | bytes 2697216 | tf_op jit(solution)/shard_map/jqk,qjd->kd/dot_general | solution.py:172
  176.2 2.5 %fusion.78 = bf16[128,128]{0,1:T(8,128)(2,1)} fusion(bf16[640,4,128]{0,2,1:T(8,128)(2,1)} %bitcast.426, f32[4,640,128]{2,1,0:T(8,128)S(1)} %fusion.25, bf16[640,4,128]{0,2,1:T(8,128)(2,1)S(1)} %bitcast.417, f32[4,640]{1,0:T(4,128)S(1)} %get-tuple-element.61, bf16[128,512]{1,0:T(8,128)(2,1)S(1)} %copy-done.11), kind=kOutput, calls=%fused_computation.110 | convolution fusion | flops 168787968 | bytes 2697216 | tf_op jit(solution)/shard_map/jqk,qjd->kd/dot_general | solution.py:172
  180.7 2.5 %fusion.77 = bf16[128,128]{0,1:T(8,128)(2,1)} fusion(bf16[640,4,128]{0,2,1:T(8,128)(2,1)} %bitcast.424, f32[4,640,128]{2,1,0:T(8,128)S(1)} %fusion.26, bf16[640,4,128]{0,2,1:T(8,128)(2,1)S(1)} %bitcast.415, f32[4,640]{1,0:T(4,128)} %get-tuple-element.62, bf16[128,512]{1,0:T(8,128)(2,1)S(1)} %copy-done.11), kind=kOutput, calls=%fused_computation.109 | convolution fusion | flops 168787968 | bytes 2697216 | tf_op jit(solution)/shard_map/jqk,qjd->kd/dot_general | solution.py:172
  (185 shorter events, 80.7 us)
Async XLA Ops:
  0.6 29.6 %collective-permute-start.4 = (bf16[128,512]{1,0:T(8,128)(2,1)}, bf16[128,512]{1,0:T(8,128)(2,1)S(1)}, u32[]{:S(2)}, u32[]{:S(2)}) collective-permute-start(bf16[128,512]{1,0:T(8,128)(2,1)} %param.6), channel_id=1, source_target_pairs={{0,4},{1,5},{2,6},{3,7},{4,8},{5,9},{6,10},{7,11},{8,12},{9,13},{1... | collective-permute-start | bytes 393224 | tf_op jit(solution)/shard_map/ppermute | solution.py:20
  5.6 27.7 %collective-permute-start.5 = (bf16[128,512]{1,0:T(8,128)(2,1)}, bf16[128,512]{1,0:T(8,128)(2,1)S(1)}, u32[]{:S(2)}, u32[]{:S(2)}) collective-permute-start(bf16[128,512]{1,0:T(8,128)(2,1)} %param.6), channel_id=1, source_target_pairs={{0,3},{1,4},{2,5},{3,6},{4,7},{5,8},{6,9},{7,10},{8,11},{9,12},{10... | collective-permute-start | bytes 393224 | tf_op jit(solution)/shard_map/ppermute | solution.py:20
  8.2 27.4 %collective-permute-start.6 = (bf16[128,512]{1,0:T(8,128)(2,1)}, bf16[128,512]{1,0:T(8,128)(2,1)S(1)}, u32[]{:S(2)}, u32[]{:S(2)}) collective-permute-start(bf16[128,512]{1,0:T(8,128)(2,1)} %param.6), channel_id=1, source_target_pairs={{0,2},{1,3},{2,4},{3,5},{4,6},{5,7},{6,8},{7,9},{8,10},{9,11},{10,... | collective-permute-start | bytes 393224 | tf_op jit(solution)/shard_map/ppermute | solution.py:20
  11.6 25.8 %collective-permute-start.7 = (bf16[128,512]{1,0:T(8,128)(2,1)}, bf16[128,512]{1,0:T(8,128)(2,1)S(1)}, u32[]{:S(2)}, u32[]{:S(2)}) collective-permute-start(bf16[128,512]{1,0:T(8,128)(2,1)} %param.6), channel_id=1, source_target_pairs={{0,1},{1,2},{2,3},{3,4},{4,5},{5,6},{6,7},{7,8},{8,9},{9,10},{10,1... | collective-permute-start | bytes 393224 | tf_op jit(solution)/shard_map/ppermute | solution.py:20
  15.3 24.2 %collective-permute-start = (bf16[128,512]{0,1:T(8,128)(2,1)S(1)}, bf16[128,512]{0,1:T(8,128)(2,1)}, u32[]{:S(2)}, u32[]{:S(2)}) collective-permute-start(bf16[128,512]{0,1:T(8,128)(2,1)S(1)} %copy.299), channel_id=1, source_target_pairs={{0,4},{1,5},{2,6},{3,7},{4,8},{5,9},{6,10},{7,11},{8,12},{9,13},{1... | collective-permute-start | bytes 393224 | tf_op jit(solution)/shard_map/ppermute | solution.py:20
  30.3 11.4 %collective-permute-start.1 = (bf16[128,512]{0,1:T(8,128)(2,1)S(1)}, bf16[128,512]{0,1:T(8,128)(2,1)S(1)}, u32[]{:S(2)}, u32[]{:S(2)}) collective-permute-start(bf16[128,512]{0,1:T(8,128)(2,1)S(1)} %copy.299), channel_id=1, source_target_pairs={{0,3},{1,4},{2,5},{3,6},{4,7},{5,8},{6,9},{7,10},{8,11},{9,12},{10... | collective-permute-start | bytes 393224 | tf_op jit(solution)/shard_map/ppermute | solution.py:20
  33.3 9.9 %collective-permute-start.2 = (bf16[128,512]{0,1:T(8,128)(2,1)S(1)}, bf16[128,512]{0,1:T(8,128)(2,1)S(1)}, u32[]{:S(2)}, u32[]{:S(2)}) collective-permute-start(bf16[128,512]{0,1:T(8,128)(2,1)S(1)} %copy.299), channel_id=1, source_target_pairs={{0,2},{1,3},{2,4},{3,5},{4,6},{5,7},{6,8},{7,9},{8,10},{9,11},{10,... | collective-permute-start | bytes 393224 | tf_op jit(solution)/shard_map/ppermute | solution.py:20
  35.6 7.6 %collective-permute-start.3 = (bf16[128,512]{0,1:T(8,128)(2,1)S(1)}, bf16[128,512]{0,1:T(8,128)(2,1)S(1)}, u32[]{:S(2)}, u32[]{:S(2)}) collective-permute-start(bf16[128,512]{0,1:T(8,128)(2,1)S(1)} %copy.299), channel_id=1, source_target_pairs={{0,1},{1,2},{2,3},{3,4},{4,5},{5,6},{6,7},{7,8},{8,9},{9,10},{10,1... | collective-permute-start | bytes 393224 | tf_op jit(solution)/shard_map/ppermute | solution.py:20
  37.4 77.7 %collective-permute-start.8 = (bf16[128,2048]{0,1:T(8,128)(2,1)}, bf16[128,2048]{0,1:T(8,128)(2,1)}, u32[]{:S(2)}, u32[]{:S(2)}) collective-permute-start(bf16[128,2048]{0,1:T(8,128)(2,1)} %copy.304), channel_id=1, source_target_pairs={{1,0},{2,1},{3,2},{4,3},{5,4},{6,5},{7,6},{8,7},{9,8},{10,9},{11,1... | collective-permute-start | bytes 1572872 | tf_op jit(solution)/shard_map/ppermute | solution.py:20
  39.5 78.1 %collective-permute-start.9 = (bf16[128,2048]{0,1:T(8,128)(2,1)}, bf16[128,2048]{0,1:T(8,128)(2,1)}, u32[]{:S(2)}, u32[]{:S(2)}) collective-permute-start(bf16[128,2048]{0,1:T(8,128)(2,1)} %copy.304), channel_id=1, source_target_pairs={{2,0},{3,1},{4,2},{5,3},{6,4},{7,5},{8,6},{9,7},{10,8},{11,9},{12,... | collective-permute-start | bytes 1572872 | tf_op jit(solution)/shard_map/ppermute | solution.py:20
  41.7 78.5 %collective-permute-start.10 = (bf16[128,2048]{0,1:T(8,128)(2,1)}, bf16[128,2048]{0,1:T(8,128)(2,1)}, u32[]{:S(2)}, u32[]{:S(2)}) collective-permute-start(bf16[128,2048]{0,1:T(8,128)(2,1)} %copy.304), channel_id=1, source_target_pairs={{3,0},{4,1},{5,2},{6,3},{7,4},{8,5},{9,6},{10,7},{11,8},{12,9},{13... | collective-permute-start | bytes 1572872 | tf_op jit(solution)/shard_map/ppermute | solution.py:20
  65.1 20.2 %collective-permute-start.20 = (f32[128,16]{1,0:T(8,128)S(1)}, f32[128,16]{1,0:T(8,128)}, u32[]{:S(2)}, u32[]{:S(2)}) collective-permute-start(f32[128,16]{1,0:T(8,128)S(1)} %reduce_sum.78), channel_id=1, source_target_pairs={{1,0},{2,1},{3,2},{4,3},{5,4},{6,5},{7,6},{8,7},{9,8},{10,9},{11,1... | collective-permute-start | bytes 24584 | tf_op jit(solution)/shard_map/ppermute | solution.py:20
  66.4 21.1 %collective-permute-start.21 = (f32[128,16]{1,0:T(8,128)S(1)}, f32[128,16]{1,0:T(8,128)}, u32[]{:S(2)}, u32[]{:S(2)}) collective-permute-start(f32[128,16]{1,0:T(8,128)S(1)} %reduce_sum.78), channel_id=1, source_target_pairs={{2,0},{3,1},{4,2},{5,3},{6,4},{7,5},{8,6},{9,7},{10,8},{11,9},{12,... | collective-permute-start | bytes 24584 | tf_op jit(solution)/shard_map/ppermute | solution.py:20
  85.3 9.4 %collective-permute-start.22 = (f32[128,16]{1,0:T(8,128)S(1)}, f32[128,16]{1,0:T(8,128)S(1)}, u32[]{:S(2)}, u32[]{:S(2)}) collective-permute-start(f32[128,16]{1,0:T(8,128)S(1)} %reduce_sum.78), channel_id=1, source_target_pairs={{3,0},{4,1},{5,2},{6,3},{7,4},{8,5},{9,6},{10,7},{11,8},{12,9},{13... | collective-permute-start | bytes 24584 | tf_op jit(solution)/shard_map/ppermute | solution.py:20
  87.5 8.6 %collective-permute-start.12 = (f32[128,16]{0,1:T(8,128)S(1)}, f32[128,16]{0,1:T(8,128)S(1)}, u32[]{:S(2)}, u32[]{:S(2)}) collective-permute-start(f32[128,16]{0,1:T(8,128)S(1)} %get-tuple-element.67), channel_id=1, source_target_pairs={{1,0},{2,1},{3,2},{4,3},{5,4},{6,5},{7,6},{8,7},{9,8},{10,9},{11,1... | collective-permute-start | bytes 24584 | tf_op jit(solution)/shard_map/ppermute | solution.py:20
  94.7 7.3 %collective-permute-start.13 = (f32[128,16]{0,1:T(8,128)S(1)}, f32[128,16]{0,1:T(8,128)S(1)}, u32[]{:S(2)}, u32[]{:S(2)}) collective-permute-start(f32[128,16]{0,1:T(8,128)S(1)} %get-tuple-element.67), channel_id=1, source_target_pairs={{2,0},{3,1},{4,2},{5,3},{6,4},{7,5},{8,6},{9,7},{10,8},{11,9},{12,... | collective-permute-start | bytes 24584 | tf_op jit(solution)/shard_map/ppermute | solution.py:20
  96.1 7.6 %collective-permute-start.14 = (f32[128,16]{0,1:T(8,128)S(1)}, f32[128,16]{0,1:T(8,128)S(1)}, u32[]{:S(2)}, u32[]{:S(2)}) collective-permute-start(f32[128,16]{0,1:T(8,128)S(1)} %get-tuple-element.67), channel_id=1, source_target_pairs={{3,0},{4,1},{5,2},{6,3},{7,4},{8,5},{9,6},{10,7},{11,8},{12,9},{13... | collective-permute-start | bytes 24584 | tf_op jit(solution)/shard_map/ppermute | solution.py:20
  102.1 10.5 %collective-permute-start.15 = (f32[128,16]{0,1:T(8,128)S(1)}, f32[128,16]{0,1:T(8,128)S(1)}, u32[]{:S(2)}, u32[]{:S(2)}) collective-permute-start(f32[128,16]{0,1:T(8,128)S(1)} %get-tuple-element.67), channel_id=1, source_target_pairs={{4,0},{5,1},{6,2},{7,3},{8,4},{9,5},{10,6},{11,7},{12,8},{13,9},{1... | collective-permute-start | bytes 24584 | tf_op jit(solution)/shard_map/ppermute | solution.py:20
  103.7 7.6 %collective-permute-start.23 = (f32[128,16]{1,0:T(8,128)S(1)}, f32[128,16]{1,0:T(8,128)S(1)}, u32[]{:S(2)}, u32[]{:S(2)}) collective-permute-start(f32[128,16]{1,0:T(8,128)S(1)} %reduce_sum.78), channel_id=1, source_target_pairs={{4,0},{5,1},{6,2},{7,3},{8,4},{9,5},{10,6},{11,7},{12,8},{13,9},{1... | collective-permute-start | bytes 24584 | tf_op jit(solution)/shard_map/ppermute | solution.py:20
  111.2 18.0 %collective-permute-start.11 = (bf16[128,2048]{0,1:T(8,128)(2,1)}, bf16[128,2048]{0,1:T(8,128)(2,1)}, u32[]{:S(2)}, u32[]{:S(2)}) collective-permute-start(bf16[128,2048]{0,1:T(8,128)(2,1)} %copy.304), channel_id=1, source_target_pairs={{4,0},{5,1},{6,2},{7,3},{8,4},{9,5},{10,6},{11,7},{12,8},{13,9},{1... | collective-permute-start | bytes 1572872 | tf_op jit(solution)/shard_map/ppermute | solution.py:20
  112.6 17.8 %collective-permute-start.16 = (bf16[128,2048]{0,1:T(8,128)(2,1)S(1)}, bf16[128,2048]{0,1:T(8,128)(2,1)S(1)}, u32[]{:S(2)}, u32[]{:S(2)}) collective-permute-start(bf16[128,2048]{0,1:T(8,128)(2,1)S(1)} %copy.320), channel_id=1, source_target_pairs={{1,0},{2,1},{3,2},{4,3},{5,4},{6,5},{7,6},{8,7},{9,8},{10,9},{11,1... | collective-permute-start | bytes 1572872 | tf_op jit(solution)/shard_map/ppermute | solution.py:20
  115.1 23.1 %collective-permute-start.17 = (bf16[128,2048]{0,1:T(8,128)(2,1)S(1)}, bf16[128,2048]{0,1:T(8,128)(2,1)S(1)}, u32[]{:S(2)}, u32[]{:S(2)}) collective-permute-start(bf16[128,2048]{0,1:T(8,128)(2,1)S(1)} %copy.320), channel_id=1, source_target_pairs={{2,0},{3,1},{4,2},{5,3},{6,4},{7,5},{8,6},{9,7},{10,8},{11,9},{12,... | collective-permute-start | bytes 1572872 | tf_op jit(solution)/shard_map/ppermute | solution.py:20
  117.6 23.7 %collective-permute-start.18 = (bf16[128,2048]{0,1:T(8,128)(2,1)S(1)}, bf16[128,2048]{0,1:T(8,128)(2,1)S(1)}, u32[]{:S(2)}, u32[]{:S(2)}) collective-permute-start(bf16[128,2048]{0,1:T(8,128)(2,1)S(1)} %copy.320), channel_id=1, source_target_pairs={{3,0},{4,1},{5,2},{6,3},{7,4},{8,5},{9,6},{10,7},{11,8},{12,9},{13... | collective-permute-start | bytes 1572872 | tf_op jit(solution)/shard_map/ppermute | solution.py:20
  120.2 47.8 %collective-permute-start.19 = (bf16[128,2048]{0,1:T(8,128)(2,1)S(1)}, bf16[128,2048]{0,1:T(8,128)(2,1)S(1)}, u32[]{:S(2)}, u32[]{:S(2)}) collective-permute-start(bf16[128,2048]{0,1:T(8,128)(2,1)S(1)} %copy.320), channel_id=1, source_target_pairs={{4,0},{5,1},{6,2},{7,3},{8,4},{9,5},{10,6},{11,7},{12,8},{13,9},{1... | collective-permute-start | bytes 1572872 | tf_op jit(solution)/shard_map/ppermute | solution.py:20
  (29 other events, 157.2 us)
where the time goes:
time: 189 us; the launch traced here: 187 us
  waiting for transfers between devices  58.6 us (31%)
  starting transfers between devices  45.8 us (24%)
  local copies, waits for them, and re-layouts  37.8 us (20%)
  matrix products  33.9 us (18%)
  other arithmetic  9.8 us (5%)
    ppermute x24, waiting for transfers between devices, passed_along(): lax.ppermute(value, axis, [(source, source + steps) for source in range(f...  58.6 us
    ppermute x24, starting transfers between devices, passed_along(): lax.ppermute(value, axis, [(source, source + steps) for source in range(f...  45.8 us
    unnamed x87, local copies, waits for them, and re-layouts  16.7 us
    dot_general x4, matrix products, body(): jnp.einsum('jqk,kd->qjd', score_grad, key_part, preferred_element_type=jn...  9.5 us
    dot_general x4, matrix products, body(): jnp.einsum('jqk,qjd->kd', score_grad, query_part, preferred_element_type=...  7.77 us
    dot_general x4, matrix products, body(): jnp.einsum('jqk,kd->qjd', weights.astype(jnp.bfloat16), head_slice(value_...  7.37 us
    dot_general x4, matrix products, score_grads(): jnp.einsum('qjd,kd->jqk', query_part, key_part, preferred_element_type=jn...  6.31 us
    reshape x4, local copies, waits for them, and re-layouts, body(): query_grad.astype(jnp.bfloat16).reshape(row_count, group_cols)  4.45 us
  transfers between devices with their start and end apart: 24, of which 8 were waited for; matrix products, arithmetic and copies ran while one was open for 33% of the time, Pallas kernels for 0%

commit v1 on v0

v1 whole, which is shorter than its diff:
```python
import functools
import math

import jax
import jax.numpy as jnp
from jax import lax
from jax.experimental import pallas as pl
from jax.experimental.pallas import tpu as pltpu
from jax.sharding import PartitionSpec as P

HEAD_WIDTH = 128
QUERY_HEADS = 16
KEY_VALUE_HEADS = 4
SPAN = 4
GROUP = QUERY_HEADS // KEY_VALUE_HEADS
MESH = pl.DeviceIdType.MESH


def dims(lhs, rhs):
    return (((lhs,), (rhs,)), ((), ()))


def dot(a, b, lhs, rhs):
    return lax.dot_general(a, b, dims(lhs, rhs), preferred_element_type=jnp.float32)


def stacked(block):
    return jnp.concatenate(
        [block[:, j * HEAD_WIDTH : (j + 1) * HEAD_WIDTH] for j in range(GROUP)], axis=0
    )


def kernel(
    count,
    lens_ref,
    q_ref,
    k_ref,
    v_ref,
    g_ref,
    o_ref,
    dq_ref,
    dk_ref,
    dv_ref,
    win,
    part,
    got,
    own,
    bias,
    kv_send,
    kv_recv,
    part_send,
    part_recv,
):
    rows = q_ref.shape[0]
    group = lax.axis_index("groups")
    me = lax.axis_index("dp")
    scale = 1.0 / math.sqrt(HEAD_WIDTH)
    window = (SPAN + 1) * rows
    width = GROUP * HEAD_WIDTH

    barrier = pltpu.get_barrier_semaphore()
    for o in range(1, SPAN + 1):

        @pl.when(me >= o)
        def _():
            pl.semaphore_signal(barrier, inc=1, device_id=(group, me - o), device_id_type=MESH)

        @pl.when(me + o < count)
        def _():
            pl.semaphore_signal(barrier, inc=1, device_id=(group, me + o), device_id_type=MESH)

    for h in range(KEY_VALUE_HEADS):
        cols = slice(h * HEAD_WIDTH, (h + 1) * HEAD_WIDTH)
        win[h, 0, SPAN] = k_ref[:, cols]
        win[h, 1, SPAN] = v_ref[:, cols]

    pl.semaphore_wait(barrier, jnp.minimum(me, SPAN) + jnp.minimum(count - 1 - me, SPAN))

    def kv_copy(h, o):
        return pltpu.make_async_remote_copy(
            src_ref=win.at[h, :, SPAN],
            dst_ref=win.at[h, :, SPAN - o],
            send_sem=kv_send.at[h, o - 1],
            recv_sem=kv_recv.at[h, o - 1],
            device_id=(group, me + o),
            device_id_type=MESH,
        )

    def part_copy(h, o):
        return pltpu.make_async_remote_copy(
            src_ref=part.at[h, o - 1],
            dst_ref=got.at[h, o - 1],
            send_sem=part_send.at[h, o - 1],
            recv_sem=part_recv.at[h, o - 1],
            device_id=(group, me - o),
            device_id_type=MESH,
        )

    for h in range(KEY_VALUE_HEADS):
        for o in range(SPAN, 0, -1):

            @pl.when(me + o < count)
            def _():
                kv_copy(h, o).start()

    for o in range(1, SPAN + 1):

        @pl.when(me < o)
        def _():
            win[:, :, SPAN - o] = jnp.zeros_like(win[:, :, SPAN - o])

        @pl.when(me + o >= count)
        def _():
            got[:, o - 1] = jnp.zeros_like(got[:, o - 1])

    q_pos = me * rows + lax.broadcasted_iota(jnp.int32, (1, rows), 1)
    begin = jnp.zeros((1, rows), jnp.int32)
    doc_end = jnp.int32(0)
    for d in range(lens_ref.shape[0]):
        doc_end = doc_end + lens_ref[d]
        begin = jnp.where(q_pos >= doc_end, doc_end, begin)
    k_pos = (me - SPAN) * rows + lax.broadcasted_iota(jnp.int32, (window, rows), 0)
    bias[...] = jnp.where((k_pos >= begin) & (k_pos <= q_pos), 0.0, -1e30)

    def head(h, carry):
        for o in range(1, SPAN + 1):

            @pl.when(me >= o)
            def _():
                kv_copy(h, o).wait_recv()

        cols = pl.ds(pl.multiple_of(h * width, width), width)
        keys = win[h, 0].reshape(window, HEAD_WIDTH)
        values = win[h, 1].reshape(window, HEAD_WIDTH)
        q4 = stacked(q_ref[:, cols])
        g4 = stacked(g_ref[:, cols])
        scores = dot(keys, q4, 1, 1) + jnp.concatenate([bias[...]] * GROUP, axis=1)
        row_max = jnp.max(scores, axis=0, keepdims=True)
        weights = jnp.exp2((scores - row_max) * (scale / math.log(2.0)))
        inverse = 1.0 / jnp.sum(weights, axis=0, keepdims=True)
        mixed = dot(values, weights.astype(jnp.bfloat16), 0, 0) * inverse
        probs = weights * inverse
        prob_grads = dot(values, g4, 1, 1)
        terms = probs * prob_grads
        deltas = jnp.sum(terms, axis=0, keepdims=True)
        ds16 = (terms - probs * deltas).astype(jnp.bfloat16)
        p16 = probs.astype(jnp.bfloat16)
        dk = dot(ds16, q4, 1, 0) * scale
        dv = dot(p16, g4, 1, 0)
        for o in range(1, SPAN + 1):
            block = slice((SPAN - o) * rows, (SPAN - o + 1) * rows)
            part[h, o - 1, 0] = dk[block].astype(jnp.bfloat16)
            part[h, o - 1, 1] = dv[block].astype(jnp.bfloat16)
        own[h, 0] = dk[SPAN * rows :]
        own[h, 1] = dv[SPAN * rows :]
        for o in range(SPAN, 0, -1):

            @pl.when(me >= o)
            def _():
                part_copy(h, o).start()

        query_grad = dot(keys, ds16, 0, 0) * scale
        for j in range(GROUP):
            span = slice(j * rows, (j + 1) * rows)
            out = pl.ds(pl.multiple_of(h * width + j * HEAD_WIDTH, HEAD_WIDTH), HEAD_WIDTH)
            o_ref[:, out] = mixed[:, span].T.astype(jnp.bfloat16)
            dq_ref[:, out] = query_grad[:, span].T.astype(jnp.bfloat16)
        return carry

    lax.fori_loop(0, KEY_VALUE_HEADS, head, 0)

    def finish(h, carry):
        for o in range(1, SPAN + 1):

            @pl.when(me + o < count)
            def _():
                part_copy(h, o).wait_recv()
                kv_copy(h, o).wait_send()

            @pl.when(me >= o)
            def _():
                part_copy(h, o).wait_send()

        total = own[h]
        for o in range(1, SPAN + 1):
            total = total + got[h, o - 1].astype(jnp.float32)
        out = pl.ds(pl.multiple_of(h * HEAD_WIDTH, HEAD_WIDTH), HEAD_WIDTH)
        dk_ref[:, out] = total[0].astype(jnp.bfloat16)
        dv_ref[:, out] = total[1].astype(jnp.bfloat16)
        return carry

    lax.fori_loop(0, KEY_VALUE_HEADS, finish, 0)


def solution(mesh):
    count = mesh.shape["dp"]

    def body(queries, key_vectors, value_vectors, output_gradient, doc_lengths):
        rows = queries.shape[0]
        vmem = pl.BlockSpec(memory_space=pltpu.VMEM)
        pair = (2, rows, HEAD_WIDTH)
        heads = KEY_VALUE_HEADS
        return pl.pallas_call(
            functools.partial(kernel, count),
            out_shape=[
                jax.ShapeDtypeStruct(a.shape, jnp.bfloat16)
                for a in (queries, queries, key_vectors, value_vectors)
            ],
            in_specs=[pl.BlockSpec(memory_space=pltpu.SMEM)] + [vmem] * 4,
            out_specs=[vmem] * 4,
            scratch_shapes=[
                pltpu.VMEM((heads, 2, SPAN + 1, rows, HEAD_WIDTH), jnp.bfloat16),
                pltpu.VMEM((heads, SPAN) + pair, jnp.bfloat16),
                pltpu.VMEM((heads, SPAN) + pair, jnp.bfloat16),
                pltpu.VMEM((heads,) + pair, jnp.float32),
                pltpu.VMEM(((SPAN + 1) * rows, rows), jnp.float32),
            ]
            + [pltpu.SemaphoreType.DMA((heads, SPAN))] * 4,
            compiler_params=pltpu.CompilerParams(
                collective_id=0, has_side_effects=True, vmem_limit_bytes=48 * 1024 * 1024
            ),
            cost_estimate=pl.CostEstimate(
                flops=10 * rows * rows * (SPAN + 1) * QUERY_HEADS * HEAD_WIDTH,
                bytes_accessed=12 * rows * QUERY_HEADS * HEAD_WIDTH,
                transcendentals=rows * rows * (SPAN + 1) * QUERY_HEADS,
            ),
        )(doc_lengths, queries, key_vectors, value_vectors, output_gradient)

    spread = P(("groups", "dp"), None)
    return jax.shard_map(
        body,
        mesh=mesh,
        in_specs=(spread,) * 4 + (P("groups"),),
        out_specs=(spread,) * 4,
        check_vma=False,
    )
```

time: 189 us -> 42.2 us (0.22)
  the two profiles are of different devices: /device:TPU:0 before, /device:TPU:13 now
where the time goes in v1:
time: 42.2 us; the launch traced here: 42 us
  Pallas kernels  33.9 us (80%)
  local copies, waits for them, and re-layouts  7.44 us (18%)
  between operations  0.65 us (2%)
    pallas_call x1, Pallas kernels, body(): pl.pallas_call(functools.partial(kernel, count), out_shape=[jax.ShapeDtyp...  33.9 us
    unnamed x14, local copies, waits for them, and re-layouts  7.44 us

profile of v1, /device:TPU:13, one launch (start us, length us, event | category | flops | bytes accessed | tf_op | source)
XLA Modules:
  0.0 42.0 jit_solution(16849788633324533953)
XLA Ops:
  0.6 0.0 copy-start
  0.6 1.0 %copy-done = bf16[128,2048]{1,0:T(8,128)(2,1)S(1)} copy-done((bf16[128,2048]{1,0:T(8,128)(2,1)S(1)}, bf16[128,2048]{1,0:T(8,128)(2,1)}, u32[]{:S(2)}) %copy-start) | copy-done | bytes 524312
  1.7 0.0 copy-start.1
  1.7 1.0 %copy-done.1 = bf16[128,2048]{1,0:T(8,128)(2,1)S(1)} copy-done((bf16[128,2048]{1,0:T(8,128)(2,1)S(1)}, bf16[128,2048]{1,0:T(8,128)(2,1)}, u32[]{:S(2)}) %copy-start.1) | copy-done | bytes 524312
  2.7 0.0 copy-start.2
  2.7 0.9 %copy-done.2 = bf16[128,512]{1,0:T(8,128)(2,1)S(1)} copy-done((bf16[128,512]{1,0:T(8,128)(2,1)S(1)}, bf16[128,512]{1,0:T(8,128)(2,1)}, u32[]{:S(2)}) %copy-start.2) | copy-done | bytes 131096
  3.6 0.0 copy-start.3
  3.6 0.9 %copy-done.3 = bf16[128,512]{1,0:T(8,128)(2,1)S(1)} copy-done((bf16[128,512]{1,0:T(8,128)(2,1)S(1)}, bf16[128,512]{1,0:T(8,128)(2,1)}, u32[]{:S(2)}) %copy-start.3) | copy-done | bytes 131096
  4.5 0.0 copy-start.4
  4.5 0.7 %copy-done.4 = s32[8]{0:T(128)S(1)} copy-done((s32[8]{0:T(128)S(1)}, s32[8]{0:T(128)}, u32[]{:S(2)}) %copy-start.4) | copy-done | bytes 56
  5.2 33.9 %shard_map.84 = (bf16[128,2048]{1,0:T(8,128)(2,1)S(1)}, bf16[128,2048]{1,0:T(8,128)(2,1)S(1)}, bf16[128,512]{1,0:T(8,128)(2,1)S(1)}, bf16[128,512]{1,0:T(8,128)(2,1)S(1)}) custom-call(s32[8]{0:T(128)S(1)} %copy-done.4, bf16[128,2048]{1,0:T(8,128)(2,1)S(1)} %copy-done, bf16[128,512]{1,0:T(8,128)(2,1)S(1)} %copy-done.2, bf16[128,512]{1,0:T(8,128)(2,1)S(1)} %copy-done.3, ...), custom_call_target="tpu_custom_call" | custom-call | flops 1677721600 | bytes 3145728 | tf_op jit(solution)/shard_map/pallas_call | solution.py:203
  39.1 0.8 %copy.13 = bf16[128,2048]{1,0:T(8,128)(2,1)} copy(bf16[128,2048]{1,0:T(8,128)(2,1)S(1)} %get-tuple-element.8) | data formatting | bytes 1048576
  39.9 0.8 %copy.14 = bf16[128,2048]{1,0:T(8,128)(2,1)} copy(bf16[128,2048]{1,0:T(8,128)(2,1)S(1)} %get-tuple-element.9) | data formatting | bytes 1048576
  40.7 0.7 %copy.15 = bf16[128,512]{1,0:T(8,128)(2,1)} copy(bf16[128,512]{1,0:T(8,128)(2,1)S(1)} %get-tuple-element.10) | data formatting | bytes 262144
  41.3 0.7 %copy.16 = bf16[128,512]{1,0:T(8,128)(2,1)} copy(bf16[128,512]{1,0:T(8,128)(2,1)S(1)} %get-tuple-element.11) | data formatting | bytes 262144
Async XLA Ops:
  0.6 1.0 %copy-start = (bf16[128,2048]{1,0:T(8,128)(2,1)S(1)}, bf16[128,2048]{1,0:T(8,128)(2,1)}, u32[]{:S(2)}) copy-start(bf16[128,2048]{1,0:T(8,128)(2,1)} %q_ref.1) | copy-start | bytes 1572868
  1.7 1.0 %copy-start.1 = (bf16[128,2048]{1,0:T(8,128)(2,1)S(1)}, bf16[128,2048]{1,0:T(8,128)(2,1)}, u32[]{:S(2)}) copy-start(bf16[128,2048]{1,0:T(8,128)(2,1)} %g_ref.1) | copy-start | bytes 1572868
  2.7 0.9 %copy-start.2 = (bf16[128,512]{1,0:T(8,128)(2,1)S(1)}, bf16[128,512]{1,0:T(8,128)(2,1)}, u32[]{:S(2)}) copy-start(bf16[128,512]{1,0:T(8,128)(2,1)} %k_ref.1) | copy-start | bytes 393220
  3.6 0.9 %copy-start.3 = (bf16[128,512]{1,0:T(8,128)(2,1)S(1)}, bf16[128,512]{1,0:T(8,128)(2,1)}, u32[]{:S(2)}) copy-start(bf16[128,512]{1,0:T(8,128)(2,1)} %v_ref.1) | copy-start | bytes 393220
  4.5 0.7 %copy-start.4 = (s32[8]{0:T(128)S(1)}, s32[8]{0:T(128)}, u32[]{:S(2)}) copy-start(s32[8]{0:T(128)} %lens_ref.1) | copy-start | bytes 100

commit v2 on v1

v2 whole, which is shorter than its diff:
```python
import functools
import math

import jax
import jax.numpy as jnp
from jax import lax
from jax.experimental import pallas as pl
from jax.experimental.pallas import tpu as pltpu
from jax.sharding import PartitionSpec as P

HEAD_WIDTH = 128
QUERY_HEADS = 16
KEY_VALUE_HEADS = 4
SPAN = 4
GROUP = QUERY_HEADS // KEY_VALUE_HEADS
MESH = pl.DeviceIdType.MESH


def dims(lhs, rhs):
    return (((lhs,), (rhs,)), ((), ()))


def dot(a, b, lhs, rhs):
    return lax.dot_general(a, b, dims(lhs, rhs), preferred_element_type=jnp.float32)


def stacked(block):
    return jnp.concatenate(
        [block[:, j * HEAD_WIDTH : (j + 1) * HEAD_WIDTH] for j in range(GROUP)], axis=0
    )


def kernel(
    count,
    lens_ref,
    q_hbm,
    k_hbm,
    v_hbm,
    g_hbm,
    o_ref,
    dq_ref,
    dk_ref,
    dv_ref,
    q_ref,
    g_ref,
    win,
    mine,
    theirs,
    keep,
    out,
    got,
    own,
    bias,
    load_sem,
    kv_sem,
    far_send,
    sib_send,
    kv_recv,
    part_send,
    part_recv,
    out_send,
    out_recv,
):
    rows = q_ref.shape[0]
    group = lax.axis_index("groups")
    me = lax.axis_index("dp")
    core = lax.rem(me, 2)
    sibling = me + 1 - 2 * core
    scale = 1.0 / math.sqrt(HEAD_WIDTH)
    window = (SPAN + 1) * rows
    width = GROUP * HEAD_WIDTH
    far = (2, 4)

    def load_kv(h):
        cols = pl.ds(h * HEAD_WIDTH, HEAD_WIDTH)
        return [
            pltpu.make_async_copy(ref.at[:, cols], win.at[h, i, SPAN], kv_sem.at[h, i])
            for i, ref in enumerate((k_hbm, v_hbm))
        ]

    load_q = pltpu.make_async_copy(q_hbm, q_ref, load_sem.at[0])
    load_g = pltpu.make_async_copy(g_hbm, g_ref, load_sem.at[1])
    for h in range(KEY_VALUE_HEADS):
        for copy in load_kv(h):
            copy.start()
    load_q.start()
    load_g.start()

    barrier = pltpu.get_barrier_semaphore()
    pl.semaphore_signal(barrier, inc=1, device_id=(group, sibling), device_id_type=MESH)
    for o in far:

        @pl.when(me >= o)
        def _():
            pl.semaphore_signal(barrier, inc=1, device_id=(group, me - o), device_id_type=MESH)

        @pl.when(me + o < count)
        def _():
            pl.semaphore_signal(barrier, inc=1, device_id=(group, me + o), device_id_type=MESH)

    for o in range(1, SPAN + 1):

        @pl.when(me < o)
        def _():
            win[:, :, SPAN - o] = jnp.zeros_like(win[:, :, SPAN - o])

    for i, o in enumerate(far):

        @pl.when(me + o >= count)
        def _():
            got[:, i] = jnp.zeros_like(got[:, i])

    q_pos = me * rows + lax.broadcasted_iota(jnp.int32, (1, rows), 1)
    begin = jnp.zeros((1, rows), jnp.int32)
    doc_end = jnp.int32(0)
    for d in range(lens_ref.shape[0]):
        doc_end = doc_end + lens_ref[d]
        begin = jnp.where(q_pos >= doc_end, doc_end, begin)
    k_pos = (me - SPAN) * rows + lax.broadcasted_iota(jnp.int32, (window, rows), 0)
    bias[...] = jnp.where((k_pos >= begin) & (k_pos <= q_pos), 0.0, -1e30)

    partners = jnp.int32(1)
    for o in far:
        partners = partners + jnp.where(me >= o, 1, 0) + jnp.where(me + o < count, 1, 0)
    pl.semaphore_wait(barrier, partners)

    def far_copy(h, i):
        return pltpu.make_async_remote_copy(
            src_ref=win.at[h, :, SPAN],
            dst_ref=win.at[h, :, SPAN - far[i]],
            send_sem=far_send.at[h, i],
            recv_sem=kv_recv.at[h, SPAN - far[i]],
            device_id=(group, me + far[i]),
            device_id_type=MESH,
        )

    def sib_copy(h, slot):
        return pltpu.make_async_remote_copy(
            src_ref=win.at[h, :, slot + 1 - 2 * core],
            dst_ref=win.at[h, :, slot],
            send_sem=sib_send.at[h, slot // 2],
            recv_sem=kv_recv.at[h, slot],
            device_id=(group, sibling),
            device_id_type=MESH,
        )

    def part_copy(h):
        return pltpu.make_async_remote_copy(
            src_ref=mine.at[h],
            dst_ref=theirs.at[h],
            send_sem=part_send.at[h],
            recv_sem=part_recv.at[h],
            device_id=(group, sibling),
            device_id_type=MESH,
        )

    def out_copy(h, i):
        return pltpu.make_async_remote_copy(
            src_ref=out.at[h, i],
            dst_ref=got.at[h, i],
            send_sem=out_send.at[h, i],
            recv_sem=out_recv.at[h, i],
            device_id=(group, me - far[i]),
            device_id_type=MESH,
        )

    for h in range(KEY_VALUE_HEADS):
        for copy in load_kv(h):
            copy.wait()
        for i in (1, 0):

            @pl.when(me + far[i] < count)
            def _():
                far_copy(h, i).start()

        @pl.when(core == 0)
        def _():
            sib_copy(h, 3).start()

    def forward(h):
        @pl.when(me >= 2)
        def _():
            far_copy(h, 0).wait_recv()

        @pl.when((me >= 2) & (core == 1))
        def _():
            sib_copy(h, 3).start()

        @pl.when(me >= 4)
        def _():
            far_copy(h, 1).wait_recv()

        @pl.when(me >= 2 + 2 * core)
        def _():
            sib_copy(h, 1).start()

    def pass_on(h):
        part_copy(h).wait_recv()
        near = keep[h, 0] + theirs[h, 1 - core].astype(jnp.float32)
        out[h, 0] = near.astype(jnp.bfloat16)
        extra = jnp.where(core == 1, theirs[h, 1].astype(jnp.float32), 0.0)
        out[h, 1] = (keep[h, 1] + extra).astype(jnp.bfloat16)
        for i in (1, 0):

            @pl.when(me >= far[i])
            def _():
                out_copy(h, i).start()

    forward(0)
    load_q.wait()
    load_g.wait()

    def head(h, carry):
        for slot in (3, 1):

            @pl.when(me >= SPAN - slot)
            def _():
                sib_copy(h, slot).wait_recv()

        cols = pl.ds(pl.multiple_of(h * width, width), width)
        keys = win[h, 0].reshape(window, HEAD_WIDTH)
        values = win[h, 1].reshape(window, HEAD_WIDTH)
        q4 = stacked(q_ref[:, cols])
        g4 = stacked(g_ref[:, cols])
        scores = dot(keys, q4, 1, 1) + jnp.concatenate([bias[...]] * GROUP, axis=1)
        row_max = jnp.max(scores, axis=0, keepdims=True)
        weights = jnp.exp2((scores - row_max) * (scale / math.log(2.0)))
        inverse = 1.0 / jnp.sum(weights, axis=0, keepdims=True)
        mixed = dot(values, weights.astype(jnp.bfloat16), 0, 0) * inverse

        @pl.when(h + 1 < KEY_VALUE_HEADS)
        def _():
            forward(h + 1)

        probs = weights * inverse
        prob_grads = dot(values, g4, 1, 1)
        terms = probs * prob_grads
        deltas = jnp.sum(terms, axis=0, keepdims=True)
        ds16 = (terms - probs * deltas).astype(jnp.bfloat16)
        p16 = probs.astype(jnp.bfloat16)
        dk = dot(ds16, q4, 1, 0) * scale
        dv = dot(p16, g4, 1, 0)
        for i, grad in enumerate((dk, dv)):
            blocks = [grad[b * rows : (b + 1) * rows] for b in range(SPAN + 1)]
            mine[h, 0, i] = blocks[3].astype(jnp.bfloat16)
            mine[h, 1, i] = blocks[1].astype(jnp.bfloat16)
            keep[h, 0, i] = blocks[2]
            keep[h, 1, i] = blocks[0]
            own[h, i] = blocks[4]
        part_copy(h).start()

        query_grad = dot(keys, ds16, 0, 0) * scale
        for j in range(GROUP):
            span = slice(j * rows, (j + 1) * rows)
            part = pl.ds(pl.multiple_of(h * width + j * HEAD_WIDTH, HEAD_WIDTH), HEAD_WIDTH)
            o_ref[:, part] = mixed[:, span].T.astype(jnp.bfloat16)
            dq_ref[:, part] = query_grad[:, span].T.astype(jnp.bfloat16)

        pass_on(h)
        return carry

    lax.fori_loop(0, KEY_VALUE_HEADS, head, 0)

    def finish(h, carry):
        for i in (0, 1):

            @pl.when(me + far[i] < count)
            def _():
                far_copy(h, i).wait_send()
                out_copy(h, i).wait_recv()

            @pl.when(me >= far[i])
            def _():
                out_copy(h, i).wait_send()

        @pl.when(me >= 2 * core)
        def _():
            sib_copy(h, 3).wait_send()

        @pl.when(me >= 2 + 2 * core)
        def _():
            sib_copy(h, 1).wait_send()

        part_copy(h).wait_send()
        total = own[h] + jnp.where(core == 0, theirs[h, 0].astype(jnp.float32), 0.0)
        for i in (0, 1):
            total = total + got[h, i].astype(jnp.float32)
        part = pl.ds(pl.multiple_of(h * HEAD_WIDTH, HEAD_WIDTH), HEAD_WIDTH)
        dk_ref[:, part] = total[0].astype(jnp.bfloat16)
        dv_ref[:, part] = total[1].astype(jnp.bfloat16)
        return carry

    lax.fori_loop(0, KEY_VALUE_HEADS, finish, 0)


def solution(mesh):
    count = mesh.shape["dp"]

    def body(queries, key_vectors, value_vectors, output_gradient, doc_lengths):
        rows = queries.shape[0]
        vmem = pl.BlockSpec(memory_space=pltpu.VMEM)
        pair = (2, rows, HEAD_WIDTH)
        heads = KEY_VALUE_HEADS
        return pl.pallas_call(
            functools.partial(kernel, count),
            out_shape=[
                jax.ShapeDtypeStruct(a.shape, jnp.bfloat16)
                for a in (queries, queries, key_vectors, value_vectors)
            ],
            in_specs=[pl.BlockSpec(memory_space=pltpu.SMEM)]
            + [pl.BlockSpec(memory_space=pltpu.HBM)] * 4,
            out_specs=[vmem] * 4,
            scratch_shapes=[
                pltpu.VMEM(queries.shape, jnp.bfloat16),
                pltpu.VMEM(queries.shape, jnp.bfloat16),
                pltpu.VMEM((heads, 2, SPAN + 1, rows, HEAD_WIDTH), jnp.bfloat16),
                pltpu.VMEM((heads, 2) + pair, jnp.bfloat16),
                pltpu.VMEM((heads, 2) + pair, jnp.bfloat16),
                pltpu.VMEM((heads, 2) + pair, jnp.float32),
                pltpu.VMEM((heads, 2) + pair, jnp.bfloat16),
                pltpu.VMEM((heads, 2) + pair, jnp.bfloat16),
                pltpu.VMEM((heads,) + pair, jnp.float32),
                pltpu.VMEM(((SPAN + 1) * rows, rows), jnp.float32),
                pltpu.SemaphoreType.DMA((2,)),
                pltpu.SemaphoreType.DMA((heads, 2)),
                pltpu.SemaphoreType.DMA((heads, 2)),
                pltpu.SemaphoreType.DMA((heads, 2)),
                pltpu.SemaphoreType.DMA((heads, SPAN)),
                pltpu.SemaphoreType.DMA((heads,)),
                pltpu.SemaphoreType.DMA((heads,)),
                pltpu.SemaphoreType.DMA((heads, 2)),
                pltpu.SemaphoreType.DMA((heads, 2)),
            ],
            compiler_params=pltpu.CompilerParams(
                collective_id=0, has_side_effects=True, vmem_limit_bytes=48 * 1024 * 1024
            ),
            cost_estimate=pl.CostEstimate(
                flops=10 * rows * rows * (SPAN + 1) * QUERY_HEADS * HEAD_WIDTH,
                bytes_accessed=12 * rows * QUERY_HEADS * HEAD_WIDTH,
                transcendentals=rows * rows * (SPAN + 1) * QUERY_HEADS,
            ),
        )(doc_lengths, queries, key_vectors, value_vectors, output_gradient)

    spread = P(("groups", "dp"), None)
    return jax.shard_map(
        body,
        mesh=mesh,
        in_specs=(spread,) * 4 + (P("groups"),),
        out_specs=(spread,) * 4,
        check_vma=False,
    )
```

time: 42.2 us -> 36.4 us (0.86)
  the two profiles are of different devices: /device:TPU:13 before, /device:TPU:0 now
where the time goes in v2:
time: 36.4 us; the launch traced here: 36.2 us
  Pallas kernels  28.1 us (77%)
  local copies, waits for them, and re-layouts  7.44 us (20%)
  between operations  0.65 us (2%)
    pallas_call x1, Pallas kernels, body(): pl.pallas_call(functools.partial(kernel, count), out_shape=[jax.ShapeDtyp...  28.1 us
    unnamed x14, local copies, waits for them, and re-layouts  7.44 us

profile of v2, /device:TPU:0, one launch (start us, length us, event | category | flops | bytes accessed | tf_op | source)
XLA Modules:
  0.0 36.2 jit_solution(15038460010733791010)
XLA Ops:
  0.6 0.0 copy-start
  0.6 1.0 %copy-done = bf16[128,2048]{1,0:T(8,128)(2,1)S(1)} copy-done((bf16[128,2048]{1,0:T(8,128)(2,1)S(1)}, bf16[128,2048]{1,0:T(8,128)(2,1)}, u32[]{:S(2)}) %copy-start) | copy-done | bytes 524312
  1.7 0.0 copy-start.1
  1.7 1.0 %copy-done.1 = bf16[128,2048]{1,0:T(8,128)(2,1)S(1)} copy-done((bf16[128,2048]{1,0:T(8,128)(2,1)S(1)}, bf16[128,2048]{1,0:T(8,128)(2,1)}, u32[]{:S(2)}) %copy-start.1) | copy-done | bytes 524312
  2.7 0.0 copy-start.2
  2.7 0.9 %copy-done.2 = bf16[128,512]{1,0:T(8,128)(2,1)S(1)} copy-done((bf16[128,512]{1,0:T(8,128)(2,1)S(1)}, bf16[128,512]{1,0:T(8,128)(2,1)}, u32[]{:S(2)}) %copy-start.2) | copy-done | bytes 131096
  3.6 0.0 copy-start.3
  3.6 0.9 %copy-done.3 = bf16[128,512]{1,0:T(8,128)(2,1)S(1)} copy-done((bf16[128,512]{1,0:T(8,128)(2,1)S(1)}, bf16[128,512]{1,0:T(8,128)(2,1)}, u32[]{:S(2)}) %copy-start.3) | copy-done | bytes 131096
  4.5 0.0 copy-start.4
  4.5 0.7 %copy-done.4 = s32[8]{0:T(128)S(1)} copy-done((s32[8]{0:T(128)S(1)}, s32[8]{0:T(128)}, u32[]{:S(2)}) %copy-start.4) | copy-done | bytes 56
  5.2 28.1 %shard_map.84 = (bf16[128,2048]{1,0:T(8,128)(2,1)S(1)}, bf16[128,2048]{1,0:T(8,128)(2,1)S(1)}, bf16[128,512]{1,0:T(8,128)(2,1)S(1)}, bf16[128,512]{1,0:T(8,128)(2,1)S(1)}) custom-call(s32[8]{0:T(128)S(1)} %copy-done.4, bf16[128,2048]{1,0:T(8,128)(2,1)S(1)} %copy-done, bf16[128,512]{1,0:T(8,128)(2,1)S(1)} %copy-done.2, bf16[128,512]{1,0:T(8,128)(2,1)S(1)} %copy-done.3, ...), custom_call_target="tpu_custom_call" | custom-call | flops 1677721600 | bytes 3145728 | tf_op jit(solution)/shard_map/pallas_call | solution.py:304
  33.3 0.8 %copy.13 = bf16[128,2048]{1,0:T(8,128)(2,1)} copy(bf16[128,2048]{1,0:T(8,128)(2,1)S(1)} %get-tuple-element.8) | data formatting | bytes 1048576
  34.1 0.8 %copy.14 = bf16[128,2048]{1,0:T(8,128)(2,1)} copy(bf16[128,2048]{1,0:T(8,128)(2,1)S(1)} %get-tuple-element.9) | data formatting | bytes 1048576
  34.8 0.7 %copy.15 = bf16[128,512]{1,0:T(8,128)(2,1)} copy(bf16[128,512]{1,0:T(8,128)(2,1)S(1)} %get-tuple-element.10) | data formatting | bytes 262144
  35.5 0.7 %copy.16 = bf16[128,512]{1,0:T(8,128)(2,1)} copy(bf16[128,512]{1,0:T(8,128)(2,1)S(1)} %get-tuple-element.11) | data formatting | bytes 262144
Async XLA Ops:
  0.6 1.0 %copy-start = (bf16[128,2048]{1,0:T(8,128)(2,1)S(1)}, bf16[128,2048]{1,0:T(8,128)(2,1)}, u32[]{:S(2)}) copy-start(bf16[128,2048]{1,0:T(8,128)(2,1)} %q_hbm.1) | copy-start | bytes 1572868
  1.7 1.0 %copy-start.1 = (bf16[128,2048]{1,0:T(8,128)(2,1)S(1)}, bf16[128,2048]{1,0:T(8,128)(2,1)}, u32[]{:S(2)}) copy-start(bf16[128,2048]{1,0:T(8,128)(2,1)} %g_hbm.1) | copy-start | bytes 1572868
  2.7 0.9 %copy-start.2 = (bf16[128,512]{1,0:T(8,128)(2,1)S(1)}, bf16[128,512]{1,0:T(8,128)(2,1)}, u32[]{:S(2)}) copy-start(bf16[128,512]{1,0:T(8,128)(2,1)} %k_hbm.1) | copy-start | bytes 393220
  3.6 0.9 %copy-start.3 = (bf16[128,512]{1,0:T(8,128)(2,1)S(1)}, bf16[128,512]{1,0:T(8,128)(2,1)}, u32[]{:S(2)}) copy-start(bf16[128,512]{1,0:T(8,128)(2,1)} %v_hbm.1) | copy-start | bytes 393220
  4.5 0.7 %copy-start.4 = (s32[8]{0:T(128)S(1)}, s32[8]{0:T(128)}, u32[]{:S(2)}) copy-start(s32[8]{0:T(128)} %lens_ref.1) | copy-start | bytes 100

commit v3 on v2

--- a/solution.py
+++ b/solution.py
@@ -37,6 +37,10 @@
     k_hbm,
     v_hbm,
     g_hbm,
+    o_hbm,
+    dq_hbm,
+    dk_hbm,
+    dv_hbm,
     o_ref,
     dq_ref,
     dk_ref,
@@ -60,6 +64,7 @@
     part_recv,
     out_send,
     out_recv,
+    store_sem,
 ):
     rows = q_ref.shape[0]
     group = lax.axis_index("groups")
@@ -206,6 +211,20 @@
             def _():
                 out_copy(h, i).start()
 
+    def store(h):
+        cols = pl.ds(pl.multiple_of(h * width, width), width)
+        return [
+            pltpu.make_async_copy(o_ref.at[:, cols], o_hbm.at[:, cols], store_sem.at[h, 0]),
+            pltpu.make_async_copy(dq_ref.at[:, cols], dq_hbm.at[:, cols], store_sem.at[h, 1]),
+        ]
+
+    def store_grads(h):
+        cols = pl.ds(pl.multiple_of(h * HEAD_WIDTH, HEAD_WIDTH), HEAD_WIDTH)
+        return [
+            pltpu.make_async_copy(dk_ref.at[:, cols], dk_hbm.at[:, cols], store_sem.at[h, 2]),
+            pltpu.make_async_copy(dv_ref.at[:, cols], dv_hbm.at[:, cols], store_sem.at[h, 3]),
+        ]
+
     forward(0)
     load_q.wait()
     load_g.wait()
@@ -231,6 +250,10 @@
         @pl.when(h + 1 < KEY_VALUE_HEADS)
         def _():
             forward(h + 1)
+
+        @pl.when(h >= 1)
+        def _():
+            pass_on(h - 1)
 
         probs = weights * inverse
         prob_grads = dot(values, g4, 1, 1)
@@ -256,10 +279,12 @@
             o_ref[:, part] = mixed[:, span].T.astype(jnp.bfloat16)
             dq_ref[:, part] = query_grad[:, span].T.astype(jnp.bfloat16)
 
-        pass_on(h)
+        for copy in store(h):
+            copy.start()
         return carry
 
     lax.fori_loop(0, KEY_VALUE_HEADS, head, 0)
+    pass_on(KEY_VALUE_HEADS - 1)
 
     def finish(h, carry):
         for i in (0, 1):
@@ -288,9 +313,33 @@
         part = pl.ds(pl.multiple_of(h * HEAD_WIDTH, HEAD_WIDTH), HEAD_WIDTH)
         dk_ref[:, part] = total[0].astype(jnp.bfloat16)
         dv_ref[:, part] = total[1].astype(jnp.bfloat16)
+        for copy in store_grads(h):
+            copy.start()
         return carry
 
     lax.fori_loop(0, KEY_VALUE_HEADS, finish, 0)
+    for h in range(KEY_VALUE_HEADS):
+        for copy in store(h) + store_grads(h):
+            copy.wait()
+
+
+def place(*refs):
+    sources, results, held, load_sem, store_sem = refs[:4], refs[4:8], refs[8:12], refs[12], refs[13]
+    loads = [
+        pltpu.make_async_copy(source, block, load_sem.at[i])
+        for i, (source, block) in enumerate(zip(sources, held))
+    ]
+    stores = [
+        pltpu.make_async_copy(block, result, store_sem.at[i])
+        for i, (block, result) in enumerate(zip(held, results))
+    ]
+    for load in loads:
+        load.start()
+    for load, store in zip(loads, stores):
+        load.wait()
+        store.start()
+    for store in stores:
+        store.wait()
 
 
 def solution(mesh):
@@ -298,19 +347,18 @@
 
     def body(queries, key_vectors, value_vectors, output_gradient, doc_lengths):
         rows = queries.shape[0]
-        vmem = pl.BlockSpec(memory_space=pltpu.VMEM)
+        hbm = pl.BlockSpec(memory_space=pl.ANY)
         pair = (2, rows, HEAD_WIDTH)
         heads = KEY_VALUE_HEADS
-        return pl.pallas_call(
+        arrays = (queries, queries, key_vectors, value_vectors)
+        shapes = [jax.ShapeDtypeStruct(a.shape, jnp.bfloat16) for a in arrays]
+        results = pl.pallas_call(
             functools.partial(kernel, count),
-            out_shape=[
-                jax.ShapeDtypeStruct(a.shape, jnp.bfloat16)
-                for a in (queries, queries, key_vectors, value_vectors)
-            ],
-            in_specs=[pl.BlockSpec(memory_space=pltpu.SMEM)]
-            + [pl.BlockSpec(memory_space=pltpu.HBM)] * 4,
-            out_specs=[vmem] * 4,
-            scratch_shapes=[
+            out_shape=shapes,
+            in_specs=[pl.BlockSpec(memory_space=pltpu.SMEM)] + [hbm] * 4,
+            out_specs=[hbm] * 4,
+            scratch_shapes=[pltpu.VMEM(a.shape, jnp.bfloat16) for a in arrays]
+            + [
                 pltpu.VMEM(queries.shape, jnp.bfloat16),
                 pltpu.VMEM(queries.shape, jnp.bfloat16),
                 pltpu.VMEM((heads, 2, SPAN + 1, rows, HEAD_WIDTH), jnp.bfloat16),
@@ -330,9 +378,10 @@
                 pltpu.SemaphoreType.DMA((heads,)),
                 pltpu.SemaphoreType.DMA((heads, 2)),
                 pltpu.SemaphoreType.DMA((heads, 2)),
+                pltpu.SemaphoreType.DMA((heads, 4)),
             ],
             compiler_params=pltpu.CompilerParams(
-                collective_id=0, has_side_effects=True, vmem_limit_bytes=48 * 1024 * 1024
+                collective_id=0, has_side_effects=True, vmem_limit_bytes=63 * 1024 * 1024
             ),
             cost_estimate=pl.CostEstimate(
                 flops=10 * rows * rows * (SPAN + 1) * QUERY_HEADS * HEAD_WIDTH,
@@ -340,6 +389,15 @@
                 transcendentals=rows * rows * (SPAN + 1) * QUERY_HEADS,
             ),
         )(doc_lengths, queries, key_vectors, value_vectors, output_gradient)
+        return pl.pallas_call(
+            place,
+            out_shape=shapes,
+            in_specs=[hbm] * 4,
+            out_specs=[hbm] * 4,
+            scratch_shapes=[pltpu.VMEM(a.shape, jnp.bfloat16) for a in arrays]
+            + [pltpu.SemaphoreType.DMA((4,))] * 2,
+            compiler_params=pltpu.CompilerParams(vmem_limit_bytes=63 * 1024 * 1024),
+        )(*results)
 
     spread = P(("groups", "dp"), None)
     return jax.shard_map(

time: 36.4 us -> 31.6 us (0.87)
  local copies, waits for them, and re-layouts: 7.44 us -> 0 us
  Pallas kernels: 28.1 us -> 30.8 us
    unnamed x14 -> x0, local copies, waits for them, and re-layouts: 7.44 us -> none
    pallas_call x1 -> x2, Pallas kernels: 28.1 us -> 30.8 us  [the longest x1 28.7 us: body(): pl.pallas_call(functools.partial(kernel, count), out_shape=shapes, in_spe...]
where the time goes in v3:
time: 31.6 us; the launch traced here: 31.5 us
  Pallas kernels  30.8 us (97%)
  between operations  0.64 us (2%)
    pallas_call x1, Pallas kernels, body(): pl.pallas_call(functools.partial(kernel, count), out_shape=shapes, in_spe...  28.7 us
    pallas_call x1, Pallas kernels, body(): pl.pallas_call(place, out_shape=shapes, in_specs=[hbm] * 4, out_specs=[hb...  2.15 us

profile of v3, /device:TPU:0, one launch (start us, length us, event | category | flops | bytes accessed | tf_op | source)
XLA Modules:
  0.0 31.5 jit_solution(8700585576524827887)
XLA Ops:
  0.6 28.7 %shard_map.84 = (bf16[128,2048]{1,0:T(8,128)(2,1)}, bf16[128,2048]{1,0:T(8,128)(2,1)}, bf16[128,512]{1,0:T(8,128)(2,1)}, bf16[128,512]{1,0:T(8,128)(2,1)}) custom-call(s32[8]{0:T(128)} %lens_ref.1, bf16[128,2048]{1,0:T(8,128)(2,1)} %q_hbm.1, bf16[128,512]{1,0:T(8,128)(2,1)} %k_hbm.1, bf16[128,512]{1,0:T(8,128)(2,1)} %v_hbm.1, bf16[128,2048]{1,0:T(8,128)(2,1)} %g_hbm.1), custom_call_target="tpu_custom_call" | custom-call | flops 1677721600 | bytes 3145728 | tf_op jit(solution)/shard_map/pallas_call | solution.py:355
  29.3 2.2 %shard_map.85 = (bf16[128,2048]{1,0:T(8,128)(2,1)}, bf16[128,2048]{1,0:T(8,128)(2,1)}, bf16[128,512]{1,0:T(8,128)(2,1)}, bf16[128,512]{1,0:T(8,128)(2,1)}) custom-call(bf16[128,2048]{1,0:T(8,128)(2,1)} %get-tuple-element.8.refs_0_, bf16[128,2048]{1,0:T(8,128)(2,1)} %get-tuple-element.9.refs_1_, bf16[128,512]{1,0:T(8,128)(2,1)} %get-tuple-element.10.refs_2_, ...), custom_call_target="tpu_custom_call" | custom-call | tf_op jit(solution)/shard_map/pallas_call | solution.py:392

commit v4 on v3

--- a/solution.py
+++ b/solution.py
@@ -169,14 +169,18 @@
             device_id_type=MESH,
         )
 
+    def send_far(h):
+        for i in (0, 1):
+
+            @pl.when(me + far[i] < count)
+            def _():
+                far_copy(h, i).start()
+
     for h in range(KEY_VALUE_HEADS):
         for copy in load_kv(h):
             copy.wait()
-        for i in (1, 0):
-
-            @pl.when(me + far[i] < count)
-            def _():
-                far_copy(h, i).start()
+        if h < 2:
+            send_far(h)
 
         @pl.when(core == 0)
         def _():
@@ -198,6 +202,10 @@
         @pl.when(me >= 2 + 2 * core)
         def _():
             sib_copy(h, 1).start()
+
+        @pl.when(h + 2 < KEY_VALUE_HEADS)
+        def _():
+            send_far(h + 2)
 
     def pass_on(h):
         part_copy(h).wait_recv()
@@ -205,7 +213,7 @@
         out[h, 0] = near.astype(jnp.bfloat16)
         extra = jnp.where(core == 1, theirs[h, 1].astype(jnp.float32), 0.0)
         out[h, 1] = (keep[h, 1] + extra).astype(jnp.bfloat16)
-        for i in (1, 0):
+        for i in (0, 1):
 
             @pl.when(me >= far[i])
             def _():

time: 31.6 us -> 31.3 us (level)
    pallas_call x1, Pallas kernels: 28.7 us -> 28.3 us  [body(): pl.pallas_call(functools.partial(kernel, count), out_shape=shapes, in_spe...]
where the time goes in v4:
time: 31.3 us; the launch traced here: 31.1 us
  Pallas kernels  30.5 us (97%)
  between operations  0.64 us (2%)
    pallas_call x1, Pallas kernels, body(): pl.pallas_call(functools.partial(kernel, count), out_shape=shapes, in_spe...  28.3 us
    pallas_call x1, Pallas kernels, body(): pl.pallas_call(place, out_shape=shapes, in_specs=[hbm] * 4, out_specs=[hb...  2.15 us

profile of v4, /device:TPU:0, one launch (start us, length us, event | category | flops | bytes accessed | tf_op | source)
XLA Modules:
  0.0 31.1 jit_solution(16179069885761210912)
XLA Ops:
  0.6 28.3 %shard_map.84 = (bf16[128,2048]{1,0:T(8,128)(2,1)}, bf16[128,2048]{1,0:T(8,128)(2,1)}, bf16[128,512]{1,0:T(8,128)(2,1)}, bf16[128,512]{1,0:T(8,128)(2,1)}) custom-call(s32[8]{0:T(128)} %lens_ref.1, bf16[128,2048]{1,0:T(8,128)(2,1)} %q_hbm.1, bf16[128,512]{1,0:T(8,128)(2,1)} %k_hbm.1, bf16[128,512]{1,0:T(8,128)(2,1)} %v_hbm.1, bf16[128,2048]{1,0:T(8,128)(2,1)} %g_hbm.1), custom_call_target="tpu_custom_call" | custom-call | flops 1677721600 | bytes 3145728 | tf_op jit(solution)/shard_map/pallas_call | solution.py:363
  29.0 2.2 %shard_map.85 = (bf16[128,2048]{1,0:T(8,128)(2,1)}, bf16[128,2048]{1,0:T(8,128)(2,1)}, bf16[128,512]{1,0:T(8,128)(2,1)}, bf16[128,512]{1,0:T(8,128)(2,1)}) custom-call(bf16[128,2048]{1,0:T(8,128)(2,1)} %get-tuple-element.8.refs_0_, bf16[128,2048]{1,0:T(8,128)(2,1)} %get-tuple-element.9.refs_1_, bf16[128,512]{1,0:T(8,128)(2,1)} %get-tuple-element.10.refs_2_, ...), custom_call_target="tpu_custom_call" | custom-call | tf_op jit(solution)/shard_map/pallas_call | solution.py:400
